TPU v7x, 32 devices: a whole 2x2x4 slice. The times are simulated.
32 devices in a mesh: dp: 8 (over z, core), seq: 4 (over y, x).
Axes of the slice: x: 2, y: 2, z: 4, core: 2. Of those that a mesh axis runs over, the one named last changes fastest.
Arguments:
- mixer_in: bfloat16 [8192, 2816], P(('dp', 'seq')), parts along dimension 0, may hold values from -92 to 92
- gate_input: bfloat16 [8192, 2560], P(('dp', 'seq')), parts along dimension 0, may hold values from -6 to 6
- step_raw: bfloat16 [8192, 40], P(('dp', 'seq')), parts along dimension 0, may hold values from -6 to 6
- lengths: int32 [24], P('dp'), parts along dimension 0, may hold values from 1 to 512, 1024 in all
- deal_order: int32 [32], P('dp'), parts along dimension 0, may hold values from 0 to 3, as said below
- conv_weight: float32 [4, 2816], replicated, may hold values from -3 to 3
- conv_bias: float32 [2816], replicated, may hold values from -3 to 3
- step_bias: float32 [40], replicated, may hold values from -4 to -1
- decay_rate: float32 [40], replicated, may hold values from 0.01 to 2
- skip_gain: float32 [40], replicated, may hold values from 0.5 to 1.5
- norm_gain: float32 [2560], replicated, may hold values from 0.5 to 1.5
Outputs:
- mixed_out: bfloat16 [8192, 2560], P(('dp', 'seq')), parts along dimension 0
- final_states: float32 [24, 2560, 128], P('dp', 'seq'), parts along dimension 0
There are 8 independent parts, one for each index of `dp`. A program takes and returns all parts, laid end to end along the dimension named above; an argument that names none is the same for every part. Nothing has to cross between parts.
Inputs may be any that keep to these rules, and one draw needn't show every extreme that they name: The prompt lengths sum to 1024 and the longest is exactly 512. `deal_order`: every sequence stretch stands in exactly one dealt slot.
All inputs are finite; a program needn't handle non-finite values.
Results may differ from a plain program's by a relative error of at most 0.005.
Values may be sent and summed in bfloat16 or wider, within the bound.
A program may use at most 128 MiB of HBM per device.

v0:
```python
import jax
import jax.numpy as jnp
from jax import lax
from jax.sharding import PartitionSpec as P

HEADS = 40
HEAD_DIM = 64
STATE = 128
KERNEL = 4
STRETCH = 256
DOCS = 3
INNER = 2560
CHANNELS = 2816


def doc_index(ends, positions):
    return jnp.sum((ends[None, :] <= positions[:, None]).astype(jnp.int32), axis=1)


def body(
    mixer_in,
    gate_input,
    step_raw,
    lengths,
    deal_order,
    conv_weight,
    conv_bias,
    step_bias,
    decay_rate,
    skip_gain,
    norm_gain,
):
    myself = lax.axis_index("seq")
    local_rows = mixer_in.shape[0]
    stretches_here = local_rows // STRETCH
    stretch_total = deal_order.shape[0]
    ends = jnp.cumsum(lengths)
    all_stretches = jnp.arange(stretch_total, dtype=jnp.int32)
    my_stretches = lax.dynamic_slice_in_dim(deal_order, myself * stretches_here, stretches_here)
    lane = jnp.arange(STRETCH, dtype=jnp.int32)
    own_doc = doc_index(
        ends, (my_stretches[:, None] * STRETCH + lane[None, :]).reshape(-1)
    ).reshape(stretches_here, STRETCH)
    prev_own = jnp.where(my_stretches > 0, doc_index(ends, my_stretches * STRETCH - 1), -1)
    blocks_in = mixer_in.reshape(stretches_here, STRETCH, CHANNELS)
    tails = blocks_in[:, STRETCH - (KERNEL - 1) :, :]
    step_blocks = step_raw.reshape(stretches_here, STRETCH, HEADS)
    step = jax.nn.softplus(step_blocks.astype(jnp.float32) + step_bias)
    log_decay = -decay_rate * step
    all_tails, all_steps = (
        lax.all_gather(tails, "seq", axis=0, tiled=True),
        lax.all_gather(step_blocks, "seq", axis=0, tiled=True),
    )
    totals = jnp.sum(
        -decay_rate * jax.nn.softplus(all_steps.astype(jnp.float32) + step_bias), axis=1
    )
    slot_map = (deal_order[:, None] == all_stretches[None, :]).astype(jnp.float32)
    packed_totals = jnp.dot(slot_map.T, totals, precision=lax.Precision.HIGHEST)
    prefix = jnp.cumsum(packed_totals, axis=0)
    base = jnp.concatenate([jnp.zeros((1, HEADS), jnp.float32), prefix[:-1]], 0)
    pick_own = (my_stretches[:, None] == all_stretches[None, :]).astype(jnp.float32)
    base_own = jnp.dot(pick_own, base, precision=lax.Precision.HIGHEST)
    running = base_own[:, None, :] + jnp.cumsum(log_decay, axis=1)
    prev_pick = (deal_order[None, :] == my_stretches[:, None] - 1).astype(jnp.bfloat16)
    prev_rows = jnp.einsum(
        "is,skc->ikc", prev_pick, all_tails, preferred_element_type=jnp.float32
    ).astype(jnp.bfloat16)
    extended = jnp.concatenate([prev_rows, blocks_in], 1)
    lead = (
        my_stretches[:, None] * STRETCH
        - (KERNEL - 1)
        + jnp.arange(KERNEL - 1, dtype=jnp.int32)[None, :]
    ).reshape(-1)
    ext_doc = jnp.concatenate(
        [doc_index(ends, lead).reshape(stretches_here, KERNEL - 1), own_doc], 1
    )
    accum = jnp.zeros((stretches_here, STRETCH, CHANNELS), jnp.float32) + conv_bias
    for offset in range(KERNEL):
        keep = (ext_doc[:, offset : offset + STRETCH] == own_doc).astype(jnp.float32)
        accum = (
            accum
            + conv_weight[offset]
            * extended[:, offset : offset + STRETCH, :].astype(jnp.float32)
            * keep[..., None]
        )
    mixed = jax.nn.silu(accum).astype(jnp.bfloat16)
    values = mixed[..., :INNER]
    input_map = mixed[..., INNER : INNER + STATE]
    output_map = mixed[..., INNER + STATE :]
    scaled = (values.astype(jnp.float32) * jnp.repeat(step, HEAD_DIM, axis=2)).astype(jnp.bfloat16)
    end_weight = jnp.exp(
        jnp.where((own_doc == own_doc[:, -1:])[..., None], running[:, -1:, :] - running, -jnp.inf)
    )
    weighted = (scaled.astype(jnp.float32) * jnp.repeat(end_weight, HEAD_DIM, axis=2)).astype(
        jnp.bfloat16
    )
    states = jnp.einsum("isk,isn->ikn", weighted, input_map, preferred_element_type=jnp.float32)
    source_pick = (deal_order[:, None] == all_stretches[None, :]).astype(jnp.float32)
    source_end = jnp.dot(source_pick, prefix, precision=lax.Precision.HIGHEST)
    source_doc = doc_index(ends, deal_order * STRETCH + STRETCH - 1)
    allowed = (deal_order[None, :] < my_stretches[:, None]) & (
        source_doc[None, :] == prev_own[:, None]
    )
    spans = jnp.exp(
        jnp.where(allowed[..., None], base_own[:, None, :] - source_end[None, :, :], -jnp.inf)
    )
    state_in = jnp.einsum(
        "ick,ckn->ikn",
        jnp.repeat(spans, HEAD_DIM, axis=2),
        lax.all_gather(states, "seq", axis=0, tiled=True),
        precision=lax.Precision.HIGHEST,
    )
    later = lane[:, None] >= lane[None, :]
    direct_gain = jnp.repeat(skip_gain, HEAD_DIM)[None, :]

    def stretch_out(inputs):
        values_c, scaled_c, keys_c, queries_c, running_c, doc_c, base_c, prev_c, state_c = inputs
        scores = jnp.dot(queries_c, keys_c.T, preferred_element_type=jnp.float32)
        same = (doc_c[:, None] == doc_c[None, :]) & later
        spans = running_c.T[:, :, None] - running_c.T[:, None, :]
        mixing = (scores[None] * jnp.exp(jnp.where(same[None], spans, -jnp.inf))).astype(
            jnp.bfloat16
        )
        within = jnp.einsum(
            "hts,shp->thp",
            mixing,
            scaled_c.reshape(STRETCH, HEADS, HEAD_DIM),
            preferred_element_type=jnp.float32,
        ).reshape(STRETCH, INNER)
        readout = jnp.dot(
            queries_c, state_c.astype(jnp.bfloat16).T, preferred_element_type=jnp.float32
        )
        carry_weight = jnp.exp(
            jnp.where((doc_c == prev_c)[:, None], running_c - base_c[None, :], -jnp.inf)
        )
        return (
            within
            + readout * jnp.repeat(carry_weight, HEAD_DIM, axis=1)
            + values_c.astype(jnp.float32) * direct_gain
        )

    outputs = lax.map(
        stretch_out,
        (values, scaled, input_map, output_map, running, own_doc, base_own, prev_own, state_in),
    )
    gated = outputs.reshape(local_rows, INNER) * jax.nn.silu(gate_input.astype(jnp.float32))
    normed = gated * lax.rsqrt(jnp.mean(gated * gated, axis=1, keepdims=True) + 1e-05) * norm_gain
    mixed_out = normed.astype(jnp.bfloat16)
    slot_numbers = jnp.arange(stretches_here, dtype=jnp.int32)

    def one_doc(document):
        last = lax.dynamic_index_in_dim(ends, document, keepdims=False) - 1
        owner = last // STRETCH
        match = my_stretches == owner
        slot = jnp.sum(jnp.where(match, slot_numbers, 0))

        def present():
            within_pos = last - owner * STRETCH
            running_c = lax.dynamic_index_in_dim(running, slot, keepdims=False)
            running_e = lax.dynamic_index_in_dim(running_c, within_pos, keepdims=False)
            doc_c = lax.dynamic_index_in_dim(own_doc, slot, keepdims=False)
            scaled_c = lax.dynamic_index_in_dim(scaled, slot, keepdims=False)
            keys_c = lax.dynamic_index_in_dim(input_map, slot, keepdims=False)
            base_c = lax.dynamic_index_in_dim(base_own, slot, keepdims=False)
            prev_c = lax.dynamic_index_in_dim(prev_own, slot, keepdims=False)
            state_c = lax.dynamic_index_in_dim(state_in, slot, keepdims=False)
            weight = jnp.exp(
                jnp.where((doc_c == document)[:, None], running_e[None, :] - running_c, -jnp.inf)
            )
            final_weighted = (
                scaled_c.astype(jnp.float32) * jnp.repeat(weight, HEAD_DIM, axis=1)
            ).astype(jnp.bfloat16)
            part = jnp.dot(final_weighted.T, keys_c, preferred_element_type=jnp.float32)
            carry_weight = jnp.exp(jnp.where(prev_c == document, running_e - base_c, -jnp.inf))
            return part + jnp.repeat(carry_weight, HEAD_DIM)[:, None] * state_c

        def absent():
            return jnp.zeros((INNER, STATE), jnp.float32)

        return lax.cond(jnp.any(match), present, absent)

    every_doc = jnp.transpose(lax.map(one_doc, jnp.arange(DOCS, dtype=jnp.int32)), (1, 0, 2))
    kept = lax.psum_scatter(
        every_doc.astype(jnp.bfloat16), "seq", scatter_dimension=0, tiled=True
    ).astype(jnp.float32)
    final_states = jnp.transpose(kept, (1, 0, 2))
    return (mixed_out, final_states)


def solution(mesh):
    return jax.shard_map(
        body,
        mesh=mesh,
        in_specs=(
            P(("dp", "seq"), None),
            P(("dp", "seq"), None),
            P(("dp", "seq"), None),
            P("dp"),
            P("dp"),
            P(),
            P(),
            P(),
            P(),
            P(),
            P(),
        ),
        out_specs=(P(("dp", "seq"), None), P("dp", "seq", None)),
        check_vma=False,
    )
```

profile of v0, /device:TPU:0, one launch (start us, length us, event | category | flops | bytes accessed | tf_op | source)
XLA Modules:
  0.0 211.3 jit_solution(7299668758811142873)
XLA Ops:
  7.9 10.2 %all-gather = bf16[1024,40]{0,1:T(8,128)(2,1)S(1)} all-gather(bf16[256,40]{0,1:T(8,128)(2,1)} %param.17), channel_id=2, replica_groups=mesh['dp'=8,'seq'=4] {'seq'}, dimensions={0}, use_global_device_ids=true | all-gather | bytes 102400 | tf_op jit(solution)/shard_map/all_gather | solution.py:52
  19.7 1.2 dynamic_slice.62
  24.9 8.2 %all_gather.9 = bf16[4,3,2816]{2,1,0:T(4,128)(2,1)S(1)} all-gather(bf16[1,3,2816]{2,1,0:T(4,128)(2,1)S(1)} %slice.76), channel_id=1, replica_groups=mesh['dp'=8,'seq'=4] {'seq'}, dimensions={0}, use_global_device_ids=true | all-gather | bytes 84480 | tf_op jit(solution)/shard_map/all_gather | solution.py:51
  35.0 1.7 broadcast_in_dim.178
  36.7 3.3 %copy.73 = f32[1,256,2560]{2,1,0:T(8,128)} copy(f32[1,256,2560]{1,2,0:T(8,128)} %bitcast.147) | data formatting | bytes 5242880 | tf_op jit(solution)/shard_map/broadcast_in_dim | solution.py:90
  45.2 1.7 broadcast_in_dim.184
  47.0 3.4 %copy.78 = f32[1,256,2560]{2,1,0:T(8,128)} copy(f32[1,256,2560]{1,2,0:T(8,128)} %bitcast.148) | data formatting | bytes 5242880 | tf_op jit(solution)/shard_map/broadcast_in_dim | solution.py:94
  50.3 2.7 %multiply_convert_fusion.2 = bf16[1,256,2816]{2,1,0:T(8,128)(2,1)S(1)} fusion(bf16[256,2816]{1,0:T(8,128)(2,1)S(1)} %copy-done.4, bf16[1,3,2816]{2,1,0:T(4,128)(2,1)S(1)} %copy.107, bf16[1,256,2816]{2,1,0:T(8,128)(2,1)S(1)} %bitcast.151, f32[2816]{0:T(1024)S(1)} %get-tuple-element.357, f32[256]{0:T(256)S(1)} %bitcast.170, f32[2816]{0:T(1024)S(1)} %get-tuple-element.358, ...), kind=kLoop, calls=%fused_computation.33 | loop fusion | flops 20905984 | bytes 4401664 | tf_op jit(solution)/shard_map/convert_element_type | solution.py:86
  55.3 1.7 fusion.25
  60.0 59.0 %all-gather.4.cloned.1.call-done = f32[10240,128]{1,0:T(8,128)} async-done(((f32[2560,128]{1,0:T(8,128)}), f32[10240,128]{1,0:T(8,128)}) %all-gather.4.cloned.1.call-update) | async-done | bytes 5242896 | tf_op jit(solution)/shard_map/all_gather | solution.py:110
  119.0 25.7 %fusion.11 = f32[2560,1,128]{2,1,0:T(1,128)} fusion(f32[4,2560,1]{0,2,1:T(1,128)S(1)} %bitcast.155, f32[4,2560,128]{2,1,0:T(8,128)} %bitcast.177), kind=kOutput, calls=%fused_computation.21 | convolution fusion | flops 15728640 | bytes 6594560 | tf_op jit(solution)/shard_map/ick,ckn->ikn/dot_general | solution.py:107
  144.8 24.7 %while.17 = (s32[]{:T(128)}, bf16[3,2560,128]{2,1,0:T(8,128)(2,1)}, s32[3]{0:T(128)S(1)}, s32[3]{0:T(128)S(1)}, s32[1]{0:T(128)}, /*index=5*/bf16[1,256,2560]{1,...) while((s32[]{:T(128)}, bf16[3,2560,128]{2,1,0:T(8,128)(2,1)}, ...), condition=%wide.region_13.14_spmd, body=%wide.region_10.13_spmd.sunk | while | flops 170742112 | bytes 7442075 | solution.py:182
  155.0 4.1 %conditional.2 = (bf16[1,2560,128]{2,1,0:T(8,128)(2,1)S(1)}) conditional(s32[]{:T(128)} %bitcast.141, () %tuple.66, (bf16[1,256,2560]{1,2,0:T(8,128)(2,1)S(1)}, s32[]{:T(128)}, s32[1,256]{1,0:T(1,128)S(1)}, s32[]{:T(128)}, s32[]{:T(128)}, /*index=5*/f32[1,256,40]{1,2,0:T(8,128)S(1)}, bf16[1,256,128]{2,1,0:T(8,128)(2,1)S(1)}, s32[1]{0:T(128)}, ...), branch_computations={%region_11.11_spmd, %region_12.12_spmd} | conditional | flops 170742096 | bytes 6130356 | solution.py:180
  157.2 1.8 fusion
  164.5 4.1 %conditional.2 = (bf16[1,2560,128]{2,1,0:T(8,128)(2,1)S(1)}) conditional(s32[]{:T(128)} %bitcast.141, () %tuple.66, (bf16[1,256,2560]{1,2,0:T(8,128)(2,1)S(1)}, s32[]{:T(128)}, s32[1,256]{1,0:T(1,128)S(1)}, s32[]{:T(128)}, s32[]{:T(128)}, /*index=5*/f32[1,256,40]{1,2,0:T(8,128)S(1)}, bf16[1,256,128]{2,1,0:T(8,128)(2,1)S(1)}, s32[1]{0:T(128)}, ...), branch_computations={%region_11.11_spmd, %region_12.12_spmd} | conditional | flops 170742096 | bytes 6130356 | solution.py:180
  166.8 1.8 fusion
  170.7 4.3 %fusion.6 = f32[40,64,256]{2,1,0:T(8,128)} fusion(bf16[256,40,64]{0,2,1:T(8,128)(2,1)S(1)} %bitcast.144, f32[40,256]{1,0:T(8,128)S(1)} %bitcast.152, f32[256,256]{1,0:T(8,128)S(1)} %fusion.36, pred[256,256]{1,0:T(8,128)(4,1)S(1)} %fusion.30), kind=kOutput, calls=%fused_computation.16 | convolution fusion | flops 346030080 | bytes 4300800 | tf_op jit(solution)/shard_map/while/body/eval_jaxpr/hts,shp->thp/dot_general | solution.py:124
  175.0 3.2 %copy.80 = f32[256,2560]{1,0:T(8,128)} copy(f32[256,2560]{0,1:T(8,128)} %bitcast.153) | data formatting | bytes 5242880 | tf_op jit(solution)/shard_map/while/body/eval_jaxpr/reshape | solution.py:129
  178.3 1.7 broadcast_in_dim.192
  180.0 3.5 %copy.79 = f32[256,2560]{1,0:T(8,128)} copy(f32[256,2560]{0,1:T(8,128)} %bitcast.149) | data formatting | bytes 5242880 | tf_op jit(solution)/shard_map/while/body/eval_jaxpr/reshape | solution.py:138
  183.7 4.6 %multiply_reduce_fusion = (f32[256]{0:T(256)S(1)}, f32[256,2560]{1,0:T(8,128)S(1)}) fusion(bf16[256,2560]{1,0:T(8,128)(2,1)S(1)} %copy-done.10, f32[2560]{0:T(1024)S(1)} %mul.239, bf16[1,256,2816]{2,1,0:T(8,128)(2,1)} %copy-done.3, f32[256,2560]{1,0:T(8,128)} %copy.80, f32[256,2560]{1,0:T(8,128)} %copy.79, f32[2560,128]{1,0:T(8,128)S(1)} %bitcast.146), kind=kOutput, calls=%fused_computation.40 | convolution fusion | flops 176619264 | bytes 11873280 | tf_op jit(solution)/shard_map/while/body/eval_jaxpr/dot_general | solution.py:130
  188.2 1.3 multiply_convert_fusion.3
  189.6 12.8 %reduce-scatter.2.cloned.1.call-done = bf16[640,3,128]{2,0,1:T(8,128)(2,1)} async-done(((bf16[2560,3,128]{2,0,1:T(8,128)(2,1)}), bf16[640,3,128]{2,0,1:T(8,128)(2,1)}) %reduce-scatter.2.cloned.1.call-update) | async-done | bytes 491536 | tf_op jit(solution)/shard_map/reduce_scatter | solution.py:183
  202.4 2.0 convert_bitcast_fusion.2
  (101 shorter events, 27.0 us)
Async XLA Ops:
  7.2 111.8 %all-gather.4.cloned.1.call-start = ((), (), s32[]{:S(2)}) async-start(), calls=%async_computation.2 | async-start | bytes 6553600 | tf_op jit(solution)/shard_map/all_gather | solution.py:110
  36.7 4.6 %copy-start.7 = (f32[40]{0:T(128)S(1)}, f32[40]{0:T(128)}, u32[]{:S(2)}) copy-start(f32[40]{0:T(128)} %param.22) | copy-start | bytes 484
  36.7 5.0 %copy-start.8 = (s32[4]{0:T(128)S(1)}, s32[4]{0:T(128)}, u32[]{:S(2)}) copy-start(s32[4]{0:T(128)} %param.19) | copy-start | bytes 52
  46.9 3.4 %copy-start.4 = (bf16[256,2816]{1,0:T(8,128)(2,1)S(1)}, bf16[256,2816]{1,0:T(8,128)(2,1)}, u32[]{:S(2)}) copy-start(bf16[256,2816]{1,0:T(8,128)(2,1)} %param.15) | copy-start | bytes 4325380
  47.0 3.4 %copy-start.6 = (f32[2816]{0:T(1024)S(1)}, f32[2816]{0:T(1024)}, u32[]{:S(2)}) copy-start(f32[2816]{0:T(1024)} %param.21) | copy-start | bytes 33796
  50.3 2.7 %copy-start.1 = (f32[1,256,2560]{2,1,0:T(8,128)S(1)}, f32[1,256,2560]{2,1,0:T(8,128)}, u32[]{:S(2)}) copy-start(f32[1,256,2560]{2,1,0:T(8,128)} %copy.73) | copy-start | bytes 7864324
  53.1 1.1 copy-start.3
  53.1 2.3 %copy-start.2 = (f32[1,256,2560]{2,1,0:T(8,128)S(1)}, f32[1,256,2560]{2,1,0:T(8,128)}, u32[]{:S(2)}) copy-start(f32[1,256,2560]{2,1,0:T(8,128)} %copy.78) | copy-start | bytes 7864324
  57.1 145.3 %reduce-scatter.2.cloned.1.call-start = ((), (), s32[]{:S(2)}) async-start(), calls=%async_computation.1 | async-start | bytes 2457600 | tf_op jit(solution)/shard_map/reduce_scatter | solution.py:183
  180.0 3.5 %copy-start.9 = (f32[40]{0:T(128)S(1)}, f32[40]{0:T(128)}, u32[]{:S(2)}) copy-start(f32[40]{0:T(128)} %param.24) | copy-start | bytes 484
  180.0 3.7 %copy-start = (f32[1,2560,128]{2,1,0:T(8,128)S(1)}, f32[1,2560,128]{2,1,0:T(8,128)}, u32[]{:S(2)}) copy-start(f32[1,2560,128]{2,1,0:T(8,128)} %get-tuple-element.528) | copy-start | bytes 3932164
  180.0 3.7 %copy-start.10 = (bf16[256,2560]{1,0:T(8,128)(2,1)S(1)}, bf16[256,2560]{1,0:T(8,128)(2,1)}, u32[]{:S(2)}) copy-start(bf16[256,2560]{1,0:T(8,128)(2,1)} %param.16) | copy-start | bytes 3932164
  183.7 4.6 %copy-start.5 = (f32[2560]{0:T(1024)S(1)}, f32[2560]{0:T(1024)}, u32[]{:S(2)}) copy-start(f32[2560]{0:T(1024)} %param.25) | copy-start | bytes 30724
Sparse Core Ops, SparseCore 0:
  57.2 61.6 all-gather.3
  169.6 32.6 reduce-scatter.1
where the time goes:
time: 213 us; the launch traced here: 211 us
  waiting for transfers between devices  71.8 us (34%)
  matrix products  43.1 us (20%)
  local copies, waits for them, and re-layouts  34.3 us (16%)
  blocking collectives  18.4 us (9%)
  between operations  16.9 us (8%)
  other arithmetic  15 us (7%)
  loops' own time  11.5 us (5%)
    all_gather x1, waiting for transfers between devices, body(): lax.all_gather(states, 'seq', axis=0, tiled=True)  59 us
    dot_general x1, matrix products, body(): jnp.einsum('ick,ckn->ikn', jnp.repeat(spans, HEAD_DIM, axis=2), lax.all_g...  25.7 us
    reduce_scatter x1, waiting for transfers between devices, body(): lax.psum_scatter(every_doc.astype(jnp.bfloat16), 'seq', scatter_dimension...  12.8 us
    all_gather x1, blocking collectives, body(): lax.all_gather(step_blocks, 'seq', axis=0, tiled=True)  10.2 us
    another operation x1, loops' own time, body(): lax.map(one_doc, jnp.arange(DOCS, dtype=jnp.int32))  9.98 us
    all_gather x1, blocking collectives, body(): lax.all_gather(tails, 'seq', axis=0, tiled=True)  8.17 us
    broadcast_in_dim x2, local copies, waits for them, and re-layouts, body(): jnp.repeat(end_weight, HEAD_DIM, axis=2)  5.07 us
    broadcast_in_dim x2, local copies, waits for them, and re-layouts, body(): jnp.repeat(step, HEAD_DIM, axis=2)  4.99 us
  transfers between devices with their start and end apart: 2, of which 2 were waited for; matrix products, arithmetic and copies ran while one was open for 11% of the time, Pallas kernels for 0%

commit v1 on v0

--- a/solution.py
+++ b/solution.py
@@ -1,6 +1,8 @@
 import jax
 import jax.numpy as jnp
 from jax import lax
+from jax.experimental import pallas as pl
+from jax.experimental.pallas import tpu as pltpu
 from jax.sharding import PartitionSpec as P
 
 HEADS = 40
@@ -15,6 +17,16 @@
 
 def doc_index(ends, positions):
     return jnp.sum((ends[None, :] <= positions[:, None]).astype(jnp.int32), axis=1)
+
+
+def lower_ones(size):
+    index = jnp.arange(size, dtype=jnp.int32)
+    return (index[:, None] >= index[None, :]).astype(jnp.float32)
+
+
+def ends_of(lengths):
+    index = jnp.arange(lengths.shape[0], dtype=jnp.int32)
+    return jnp.sum(jnp.where(index[:, None] >= index[None, :], lengths[None, :], 0), axis=1)
 
 
 def body(
@@ -34,7 +46,7 @@
     local_rows = mixer_in.shape[0]
     stretches_here = local_rows // STRETCH
     stretch_total = deal_order.shape[0]
-    ends = jnp.cumsum(lengths)
+    ends = ends_of(lengths)
     all_stretches = jnp.arange(stretch_total, dtype=jnp.int32)
     my_stretches = lax.dynamic_slice_in_dim(deal_order, myself * stretches_here, stretches_here)
     lane = jnp.arange(STRETCH, dtype=jnp.int32)
@@ -56,11 +68,13 @@
     )
     slot_map = (deal_order[:, None] == all_stretches[None, :]).astype(jnp.float32)
     packed_totals = jnp.dot(slot_map.T, totals, precision=lax.Precision.HIGHEST)
-    prefix = jnp.cumsum(packed_totals, axis=0)
+    prefix = jnp.dot(lower_ones(stretch_total), packed_totals, precision=lax.Precision.HIGHEST)
     base = jnp.concatenate([jnp.zeros((1, HEADS), jnp.float32), prefix[:-1]], 0)
     pick_own = (my_stretches[:, None] == all_stretches[None, :]).astype(jnp.float32)
     base_own = jnp.dot(pick_own, base, precision=lax.Precision.HIGHEST)
-    running = base_own[:, None, :] + jnp.cumsum(log_decay, axis=1)
+    running = base_own[:, None, :] + jnp.einsum(
+        "ts,ish->ith", lower_ones(STRETCH), log_decay, precision=lax.Precision.HIGHEST
+    )
     prev_pick = (deal_order[None, :] == my_stretches[:, None] - 1).astype(jnp.bfloat16)
     prev_rows = jnp.einsum(
         "is,skc->ikc", prev_pick, all_tails, preferred_element_type=jnp.float32
@@ -187,9 +201,479 @@
     return (mixed_out, final_states)
 
 
+GROUP = 4
+QUARTER = INNER // GROUP
+SLOT = QUARTER + STATE
+PAD = 48
+ROWS3 = 3 * PAD
+LOG2E = 1.4426950408889634
+F32 = jnp.float32
+BF16 = jnp.bfloat16
+
+
+def tn(a, b):
+    return lax.dot_general(a, b, (((0,), (0,)), ((), ())), preferred_element_type=F32)
+
+
+def nt(a, b):
+    return lax.dot_general(a, b, (((1,), (1,)), ((), ())), preferred_element_type=F32)
+
+
+def split3(a):
+    high = a.astype(BF16)
+    rest = a - high.astype(F32)
+    middle = rest.astype(BF16)
+    low = (rest - middle.astype(F32)).astype(BF16)
+    return jnp.concatenate([high, middle, low], 0)
+
+
+def head_row(shape):
+    row = lax.broadcasted_iota(jnp.int32, shape, 0)
+    return row - PAD * (row >= PAD).astype(jnp.int32) - PAD * (row >= 2 * PAD).astype(jnp.int32)
+
+
+def silu(v):
+    return v / (1.0 + jnp.exp(-v))
+
+
+def softplus(v):
+    u = jnp.exp(-jnp.abs(v))
+    small = u * (1.0 + u * (-1.0 / 2 + u * (1.0 / 3 + u * (-1.0 / 4 + u * (1.0 / 5)))))
+    return jnp.maximum(v, 0.0) + jnp.where(u < 0.03, small, jnp.log(1.0 + u))
+
+
+def one_if(condition):
+    return jnp.where(condition, 1.0, 0.0).astype(F32)
+
+
+def kernel(
+    deal,
+    lengths,
+    x,
+    gate,
+    step_raw,
+    conv_weight,
+    conv_bias,
+    heads_in,
+    norm_gain,
+    out,
+    finals,
+    steps,
+    tails,
+    keys_raw,
+    values_raw,
+    states_in,
+    staged,
+    tail_f,
+    lead,
+    ext,
+    mixed,
+    masked_scores,
+    y,
+    slot_ext,
+    slot_weighted,
+    ends_state,
+    trail,
+    carried,
+    log_run,
+    step_t,
+    weight_t,
+    split_run,
+    expand,
+    keep_mask,
+    send_sem,
+    recv_sem,
+):
+    me = lax.axis_index("seq")
+    partners = (3 - me, me + 1 - 2 * lax.rem(me, 2), lax.rem(me + 2, 4))
+    barrier = pltpu.get_barrier_semaphore()
+    for peer in partners:
+        pl.semaphore_signal(
+            barrier, inc=1, device_id={"seq": peer}, device_id_type=pl.DeviceIdType.MESH
+        )
+
+    eye = (
+        lax.broadcasted_iota(jnp.int32, (PAD, HEADS), 0)
+        == lax.broadcasted_iota(jnp.int32, (PAD, HEADS), 1)
+    ).astype(BF16)
+    steps[me] = nt(eye, step_raw[...]).astype(BF16)
+    last = x[STRETCH - 16 :, :].astype(F32)[13:16, :]
+    tail_f[0] = jnp.zeros((16, QUARTER), F32)
+    for j in range(GROUP):
+        tail_f[0, 3 * j : 3 * j + 3, :] = last[:, j * QUARTER : (j + 1) * QUARTER]
+    tail_f[0, 12:15, 0 : 2 * STATE] = last[:, INNER:]
+    tails[me] = tail_f[0].astype(BF16)
+    pl.semaphore_wait(barrier, 3)
+
+    def remote(kind, src, dst, peer, where):
+        return pltpu.make_async_remote_copy(
+            src_ref=src,
+            dst_ref=dst,
+            send_sem=send_sem.at[kind, where],
+            recv_sem=recv_sem.at[kind, me],
+            device_id={"seq": peer},
+            device_id_type=pl.DeviceIdType.MESH,
+        )
+
+    sends = []
+    for r, peer in enumerate(partners):
+        sends.append(remote(0, steps.at[me], steps.at[me], peer, r))
+        sends.append(remote(1, tails.at[me], tails.at[me], peer, r))
+    for r, peer in enumerate(partners):
+        sends.append(
+            remote(2, x.at[:, pl.ds(INNER, STATE)], keys_raw.at[me], peer, r)
+        )
+        columns = pl.ds(pl.multiple_of(peer * QUARTER, 128), QUARTER)
+        sends.append(remote(3, x.at[:, columns], values_raw.at[me], peer, r))
+    for copy in sends:
+        copy.start()
+
+    def arrived(kind, buffer, slot):
+        pltpu.make_async_remote_copy(
+            src_ref=buffer.at[slot],
+            dst_ref=buffer.at[slot],
+            send_sem=send_sem.at[kind, 0],
+            recv_sem=recv_sem.at[kind, slot],
+            device_id={"seq": slot},
+            device_id_type=pl.DeviceIdType.MESH,
+        ).wait_recv()
+
+    ends = []
+    total = 0
+    for d in range(DOCS):
+        total = total + lengths[d]
+        ends.append(total)
+
+    def doc_of(position):
+        found = 0
+        for end in ends:
+            found = found + (end <= position).astype(jnp.int32)
+        return found
+
+    order = [deal[i] for i in range(GROUP)]
+    mine = deal[me]
+
+    def prev_of(stretch):
+        return jnp.where(stretch > 0, doc_of(stretch * STRETCH - 1), -1)
+
+    prev_docs = [prev_of(s) for s in order]
+    end_docs = [doc_of(s * STRETCH + STRETCH - 1) for s in order]
+
+    def make_keep(stretch):
+        rows = lax.broadcasted_iota(jnp.int32, (STRETCH, 128), 0) + stretch * STRETCH
+        here = doc_of(rows)
+        for j in range(KERNEL - 1):
+            before = rows - (KERNEL - 1) + j
+            keep_mask[j] = one_if((doc_of(before) == here) & (before >= 0))
+        return here
+
+    columns_head = lax.broadcasted_iota(jnp.int32, (ROWS3, INNER), 1)
+    rows_head = head_row((ROWS3, INNER)) * HEAD_DIM
+    expand[...] = one_if(
+        (columns_head >= rows_head) & (columns_head < rows_head + HEAD_DIM)
+    ).astype(BF16)
+
+    quarter = pl.ds(pl.multiple_of(me * QUARTER, 128), QUARTER)
+    keys_raw[me] = x[:, INNER : INNER + STATE]
+    values_raw[me] = x[:, quarter]
+
+    for r, peer in enumerate(partners):
+        arrived(0, steps, peer)
+        arrived(1, tails, peer)
+    for i in range(GROUP):
+        tail_f[i] = tails[i].astype(F32)
+    for i in range(GROUP):
+        total_tail = jnp.zeros((16, QUARTER), F32)
+        for j in range(GROUP):
+            if j != i:
+                total_tail = total_tail + one_if(order[j] == order[i] - 1) * tail_f[j]
+        lead[i] = total_tail
+
+    step_bias = heads_in[:, 0:1]
+    rate = heads_in[:, 1:2] * LOG2E
+    upper = one_if(
+        lax.broadcasted_iota(jnp.int32, (STRETCH, STRETCH), 0)
+        <= lax.broadcasted_iota(jnp.int32, (STRETCH, STRETCH), 1)
+    ).astype(BF16)
+    lanes = lax.broadcasted_iota(jnp.int32, (PAD, STRETCH), 1)
+    totals = []
+    at_end = []
+    for i in range(GROUP):
+        step = softplus(steps[i].astype(F32) + step_bias)
+        step_t[i] = step
+        sums = jnp.dot(split3(-rate * step), upper, preferred_element_type=F32)
+        run = sums[:PAD] + sums[PAD : 2 * PAD] + sums[2 * PAD :]
+        log_run[i] = run
+        totals.append(run[:, STRETCH - 1 : STRETCH])
+        doc_lane = doc_of(lanes + order[i] * STRETCH)
+        goal = jnp.zeros((PAD, STRETCH), F32)
+        row_ends = []
+        for d in range(DOCS):
+            final = jnp.minimum(ends[d] - 1 - order[i] * STRETCH, STRETCH - 1)
+            value = jnp.sum(jnp.where(lanes == final, run, 0.0), axis=1, keepdims=True)
+            row_ends.append(value)
+            goal = jnp.where(doc_lane == d, value, goal)
+        at_end.append(row_ends)
+        weight_t[i] = jnp.exp2(jnp.minimum(goal - run, 0.0))
+    split_run[...] = split3(log_run[me])
+
+    make_keep(mine)
+    for j in range(GROUP):
+        ext[5:8, j * QUARTER : (j + 1) * QUARTER] = lead[me, 3 * j : 3 * j + 3, :]
+    ext[5:8, INNER:] = lead[me, 12:15, 0 : 2 * STATE]
+
+    def conv(source, cols, weight_cols):
+        taps = conv_weight[:, weight_cols]
+        value = conv_bias[:, weight_cols] + taps[KERNEL - 1 : KERNEL] * source[8 : 8 + STRETCH, cols]
+        for j in range(KERNEL - 1):
+            value = value + taps[j : j + 1] * source[5 + j : 5 + j + STRETCH, cols] * keep_mask[j]
+        return silu(value).astype(BF16)
+
+    def own_chunk(c, carry):
+        cols = pl.ds(pl.multiple_of(c * 128, 128), 128)
+        ext[8 : 8 + STRETCH, cols] = x[:, cols].astype(F32)
+        mixed[:, cols] = conv(ext, cols, cols)
+        return carry
+
+    lax.fori_loop(0, CHANNELS // 128, own_chunk, 0)
+
+    step_rows = jnp.transpose(split3(step_t[me]).astype(F32)).astype(BF16)
+    keys = mixed[:, INNER : INNER + STATE]
+    queries = mixed[:, INNER + STATE :]
+    t_index = lax.broadcasted_iota(jnp.int32, (STRETCH, STRETCH), 0)
+    s_index = lax.broadcasted_iota(jnp.int32, (STRETCH, STRETCH), 1)
+    same = (t_index >= s_index) & (
+        doc_of(t_index + mine * STRETCH) == doc_of(s_index + mine * STRETCH)
+    )
+    scores = jnp.where(same, nt(queries, keys), 0.0)
+    low_lane = lax.broadcasted_iota(jnp.int32, (STRETCH, 128), 1) < HEAD_DIM
+    run_rows = jnp.transpose(split_run[...].astype(F32)).astype(BF16)
+    pick_rows = head_row((ROWS3, 128))
+
+    def pair(p, carry):
+        cols = pl.ds(pl.multiple_of(p * 128, 128), 128)
+        values = mixed[:, cols].astype(F32)
+        spread = expand[:, cols]
+        wide = (values * jnp.dot(step_rows, spread, preferred_element_type=F32)).astype(BF16)
+        parts = []
+        for k in range(2):
+            head = 2 * p + k
+            pick = one_if(pick_rows == head).astype(BF16)
+            column = jnp.dot(run_rows, pick, preferred_element_type=F32)
+            row = log_run[me, pl.ds(head, 1), :]
+            first = masked_scores[0:128, 0:128] * jnp.exp2(
+                jnp.minimum(column[0:128] - row[:, 0:128], 0.0)
+            )
+            top = jnp.dot(first.astype(BF16), wide[0:128], preferred_element_type=F32)
+            second = jnp.concatenate(
+                [
+                    masked_scores[128:256, b * 128 : b * 128 + 128]
+                    * jnp.exp2(
+                        jnp.minimum(column[128:256] - row[:, b * 128 : b * 128 + 128], 0.0)
+                    )
+                    for b in range(2)
+                ],
+                1,
+            )
+            bottom = jnp.dot(second.astype(BF16), wide, preferred_element_type=F32)
+            parts.append(jnp.concatenate([top, bottom], 0))
+        skip = jnp.dot(skip_rows, spread, preferred_element_type=F32)[0:1]
+        y[:, cols] = jnp.where(low_lane, parts[0], parts[1]) + skip * values
+        return carry
+
+    skip_split = split3(jnp.broadcast_to(heads_in[:, 2:3], (PAD, 128)))
+    skip_rows = jnp.transpose(skip_split.astype(F32))[0:16].astype(BF16)
+    masked_scores[...] = scores
+    lax.fori_loop(0, HEADS // 2, pair, 0)
+
+    spread_q = expand[:, quarter]
+    for slot in (me,) + (partners[1], partners[2], partners[0]):
+        if slot is not me:
+            arrived(2, keys_raw, slot)
+            arrived(3, values_raw, slot)
+        stretch = deal[slot]
+        here_slot = make_keep(stretch)
+        for k in range(KERNEL - 1):
+            slot_ext[5 + k : 6 + k, 0:QUARTER] = lead[slot, pl.ds(3 * me + k, 1), :]
+        slot_ext[5:8, QUARTER:] = lead[slot, 12:15, 0:STATE]
+        slot_ext[8:, QUARTER:] = keys_raw[slot].astype(F32)
+        slot_keys = conv(
+            slot_ext, pl.ds(QUARTER, STATE), pl.ds(INNER, STATE)
+        )
+        step_here = jnp.transpose(split3(step_t[slot]).astype(F32)).astype(BF16)
+        weight_here = jnp.transpose(split3(weight_t[slot]).astype(F32)).astype(BF16)
+
+        def slot_chunk(c, carry):
+            cols = pl.ds(pl.multiple_of(c * 128, 128), 128)
+            full = pl.ds(pl.multiple_of(me * QUARTER + c * 128, 128), 128)
+            slot_ext[8:, cols] = values_raw[slot, :, cols].astype(F32)
+            values = conv(slot_ext, cols, full).astype(F32)
+            spread = expand[:, full]
+            wide = (
+                values * jnp.dot(step_here, spread, preferred_element_type=F32)
+            ).astype(BF16)
+            slot_weighted[:, cols] = (
+                wide.astype(F32) * jnp.dot(weight_here, spread, preferred_element_type=F32)
+            ).astype(BF16)
+            return carry
+
+        lax.fori_loop(0, QUARTER // 128, slot_chunk, 0)
+        final_doc = doc_of(stretch * STRETCH + STRETCH - 1)
+        slot_keys = slot_keys.astype(F32)
+        masked = jnp.concatenate(
+            [(slot_keys * one_if(here_slot == d)).astype(BF16) for d in range(DOCS)]
+            + [(slot_keys * one_if(here_slot == final_doc)).astype(BF16)],
+            1,
+        )
+        result = tn(slot_weighted[...], masked)
+        for d in range(DOCS):
+            ends_state[slot, d] = result[:, d * STATE : (d + 1) * STATE]
+        trail[slot] = result[:, DOCS * STATE :]
+
+    lane = lax.broadcasted_iota(jnp.int32, (PAD, 128), 1)
+    weights = jnp.zeros((PAD, 128), F32)
+    for c in range(GROUP):
+        for e in range(GROUP):
+            if e == c:
+                continue
+            span = jnp.zeros((PAD, 1), F32)
+            for m in range(GROUP):
+                if m not in (c, e):
+                    span = span + one_if((order[m] > order[e]) & (order[m] < order[c])) * totals[m]
+            allowed = one_if((order[e] < order[c]) & (end_docs[e] == prev_docs[c]))
+            weights = jnp.where(lane == c * GROUP + e, allowed * jnp.exp2(span), weights)
+    for d in range(DOCS):
+        value = jnp.zeros((PAD, 1), F32)
+        for c in range(GROUP):
+            ends_here = (ends[d] > order[c] * STRETCH) & (ends[d] <= order[c] * STRETCH + STRETCH)
+            value = value + one_if(ends_here & (prev_docs[c] == d)) * jnp.exp2(at_end[c][d])
+        weights = jnp.where(lane == GROUP * GROUP + d, value, weights)
+    by_row = tn(spread_q, split3(weights))
+    for c in range(GROUP):
+        state = jnp.zeros((QUARTER, STATE), F32)
+        for e in range(GROUP):
+            if e != c:
+                state = state + by_row[:, c * GROUP + e : c * GROUP + e + 1] * trail[e]
+        carried[c] = state
+        staged[c] = state.astype(BF16)
+    back = [
+        remote(4, staged.at[peer], states_in.at[me], peer, r) for r, peer in enumerate(partners)
+    ]
+    for copy in back:
+        copy.start()
+    states_in[me] = staged[me]
+    for d in range(DOCS):
+        state = jnp.zeros((QUARTER, STATE), F32)
+        inflow = jnp.zeros((QUARTER, STATE), F32)
+        for c in range(GROUP):
+            ends_here = one_if(
+                (ends[d] > order[c] * STRETCH) & (ends[d] <= order[c] * STRETCH + STRETCH)
+            )
+            state = state + ends_here * ends_state[c, d]
+            inflow = inflow + ends_here * carried[c]
+        finals[d] = state + by_row[:, GROUP * GROUP + d : GROUP * GROUP + d + 1] * inflow
+
+    doc_lane = doc_of(lanes + mine * STRETCH)
+    carry_t = jnp.where(doc_lane == prev_of(mine), jnp.exp2(log_run[me]), 0.0)
+    carry_rows = jnp.transpose(split3(carry_t).astype(F32)).astype(BF16)
+    square = jnp.zeros((STRETCH, 128), F32)
+    for slot in (me,) + (partners[1], partners[2], partners[0]):
+        if slot is not me:
+            arrived(4, states_in, slot)
+
+        def read_chunk(c, square):
+            cols = pl.ds(pl.multiple_of(slot * QUARTER + c * 128, 128), 128)
+            rows = pl.ds(pl.multiple_of(c * 128, 128), 128)
+            readout = nt(mixed[:, INNER + STATE :], states_in[slot, rows, :])
+            carry = jnp.dot(carry_rows, expand[:, cols], preferred_element_type=F32)
+            gated = (y[:, cols] + readout * carry) * silu(gate[:, cols].astype(F32))
+            y[:, cols] = gated
+            return square + gated * gated
+
+        square = lax.fori_loop(0, QUARTER // 128, read_chunk, square)
+    mean = jnp.sum(square, axis=1, keepdims=True) * (1.0 / INNER)
+    factor = jnp.broadcast_to(lax.rsqrt(mean + 1e-05), (STRETCH, 128))
+
+    def norm_chunk(c, carry):
+        cols = pl.ds(pl.multiple_of(c * 128, 128), 128)
+        out[:, cols] = (y[:, cols] * factor * norm_gain[:, cols]).astype(BF16)
+        return carry
+
+    lax.fori_loop(0, INNER // 128, norm_chunk, 0)
+    for copy in sends + back:
+        copy.wait_send()
+
+
+def fused(
+    mixer_in,
+    gate_input,
+    step_raw,
+    lengths,
+    deal_order,
+    conv_weight,
+    conv_bias,
+    step_bias,
+    decay_rate,
+    skip_gain,
+    norm_gain,
+):
+    heads_in = jnp.pad(jnp.stack([step_bias, decay_rate, skip_gain], 1), ((0, PAD - HEADS), (0, 0)))
+    smem = pl.BlockSpec(memory_space=pltpu.SMEM)
+    vmem = pl.BlockSpec(memory_space=pltpu.VMEM)
+    return pl.pallas_call(
+        kernel,
+        out_shape=(
+            jax.ShapeDtypeStruct((STRETCH, INNER), BF16),
+            jax.ShapeDtypeStruct((DOCS, QUARTER, STATE), F32),
+        ),
+        in_specs=[smem, smem] + [vmem] * 7,
+        out_specs=(vmem, vmem),
+        scratch_shapes=[
+            pltpu.VMEM((GROUP, PAD, STRETCH), BF16),
+            pltpu.VMEM((GROUP, 16, QUARTER), BF16),
+            pltpu.VMEM((GROUP, STRETCH, STATE), BF16),
+            pltpu.VMEM((GROUP, STRETCH, QUARTER), BF16),
+            pltpu.VMEM((GROUP, QUARTER, STATE), BF16),
+            pltpu.VMEM((GROUP, QUARTER, STATE), BF16),
+            pltpu.VMEM((GROUP, 16, QUARTER), F32),
+            pltpu.VMEM((GROUP, 16, QUARTER), F32),
+            pltpu.VMEM((STRETCH + 8, CHANNELS), F32),
+            pltpu.VMEM((STRETCH, CHANNELS), BF16),
+            pltpu.VMEM((STRETCH, STRETCH), F32),
+            pltpu.VMEM((STRETCH, INNER), F32),
+            pltpu.VMEM((STRETCH + 8, SLOT), F32),
+            pltpu.VMEM((STRETCH, QUARTER), BF16),
+            pltpu.VMEM((GROUP, DOCS, QUARTER, STATE), F32),
+            pltpu.VMEM((GROUP, QUARTER, STATE), F32),
+            pltpu.VMEM((GROUP, QUARTER, STATE), F32),
+            pltpu.VMEM((GROUP, PAD, STRETCH), F32),
+            pltpu.VMEM((GROUP, PAD, STRETCH), F32),
+            pltpu.VMEM((GROUP, PAD, STRETCH), F32),
+            pltpu.VMEM((ROWS3, STRETCH), BF16),
+            pltpu.VMEM((ROWS3, INNER), BF16),
+            pltpu.VMEM((KERNEL - 1, STRETCH, 128), F32),
+            pltpu.SemaphoreType.DMA((5, GROUP)),
+            pltpu.SemaphoreType.DMA((5, GROUP)),
+        ],
+        compiler_params=pltpu.CompilerParams(
+            collective_id=0, has_side_effects=True, vmem_limit_bytes=56 * 1024 * 1024
+        ),
+    )(
+        deal_order,
+        lengths,
+        mixer_in,
+        gate_input,
+        step_raw,
+        conv_weight,
+        conv_bias[None, :],
+        heads_in,
+        norm_gain[None, :],
+    )
+
+
 def solution(mesh):
     return jax.shard_map(
-        body,
+        fused if mesh.shape["seq"] == GROUP else body,
         mesh=mesh,
         in_specs=(
             P(("dp", "seq"), None),

time: 213 us -> 63.9 us (0.30)
  waiting for transfers between devices: 71.8 us -> 0 us
  Pallas kernels: 0 us -> 53.9 us
  matrix products: 43.1 us -> 0 us
  local copies, waits for them, and re-layouts: 34.3 us -> 8.27 us
  blocking collectives: 18.4 us -> 0 us
  between operations: 16.9 us -> 0.65 us
  other arithmetic: 15 us -> 0.7 us
  loops' own time: 11.5 us -> 0 us
    all_gather x1 -> x0, waiting for transfers between devices: 59 us -> none  [body(): lax.all_gather(states, 'seq', axis=0, tiled=True)]
    pallas_call x0 -> x1, Pallas kernels: none -> 53.9 us  [fused(): pl.pallas_call(kernel, out_shape=(jax.ShapeDtypeStruct((STRETCH, INNER),...]
    dot_general x11 -> x0, matrix products: 43.1 us -> none  [the longest x1 25.7 us: body(): jnp.einsum('ick,ckn->ikn', jnp.repeat(spans, HEAD_DIM, axis=2), lax.all_g...]
    all_gather x2 -> x0, blocking collectives: 18.4 us -> none  [the longest x1 10.2 us: body(): lax.all_gather(step_blocks, 'seq', axis=0, tiled=True)]
    reduce_scatter x1 -> x0, waiting for transfers between devices: 12.8 us -> none  [body(): lax.psum_scatter(every_doc.astype(jnp.bfloat16), 'seq', scatter_dimension...]
    another operation x4 -> x0, loops' own time: 11.5 us -> none  [the longest x1 9.98 us: body(): lax.map(one_doc, jnp.arange(DOCS, dtype=jnp.int32))]
    broadcast_in_dim x10 -> x2, local copies, waits for them, and re-layouts: 12.2 us -> 2.61 us  [the longest x1 1.31 us: fused(): norm_gain[None, :]]
    reshape x2 -> x0, local copies, waits for them, and re-layouts: 6.72 us -> none  [the longest x1 3.5 us: stretch_out(): jnp.repeat(carry_weight, HEAD_DIM, axis=1)]
  transfers between devices with their start and end apart: 2 -> 0, of which waited for: 2 -> 0; matrix products, arithmetic and copies ran while one was open for 11% -> 0% of each run, Pallas kernels for 0% -> 0%
where the time goes in v1:
time: 63.9 us; the launch traced here: 63.6 us
  Pallas kernels  53.9 us (84%)
  local copies, waits for them, and re-layouts  8.27 us (13%)
  other arithmetic  0.7 us (1%)
  between operations  0.65 us (1%)
    pallas_call x1, Pallas kernels, fused(): pl.pallas_call(kernel, out_shape=(jax.ShapeDtypeStruct((STRETCH, INNER),...  53.9 us
    unnamed x5, local copies, waits for them, and re-layouts  4.95 us
    broadcast_in_dim x1, local copies, waits for them, and re-layouts, fused(): norm_gain[None, :]  1.31 us
    broadcast_in_dim x1, local copies, waits for them, and re-layouts, fused(): conv_bias[None, :]  1.31 us

profile of v1, /device:TPU:0, one launch (start us, length us, event | category | flops | bytes accessed | tf_op | source)
XLA Modules:
  0.0 63.6 jit_solution(14677888506567461695)
XLA Ops:
  0.6 0.7 %pad_maximum_fusion = f32[40,3]{0,1:T(4,128)S(1)} fusion(f32[40,1]{0,1:T(1,128)} %bitcast.3, f32[40,1]{0,1:T(1,128)} %bitcast.4, f32[40,1]{0,1:T(1,128)} %bitcast.5), kind=kLoop, calls=%fused_computation | loop fusion | flops 240 | bytes 960 | tf_op jit(solution)/shard_map/stack | solution.py:620
  1.3 1.3 %broadcast_in_dim.7.norm_gain = f32[1,2560]{1,0:T(1,128)} reshape(f32[2560]{0:T(1024)} %param.21) | data formatting | bytes 20480 | tf_op jit(solution)/shard_map/broadcast_in_dim | solution.py:670
  2.6 1.3 %broadcast_in_dim.6.conv_bias = f32[1,2816]{1,0:T(1,128)} reshape(f32[2816]{0:T(1024)} %param.17) | data formatting | bytes 22528 | tf_op jit(solution)/shard_map/broadcast_in_dim | solution.py:668
  3.9 0.1 copy.17
  4.0 0.6 pad.4.heads_in
  4.6 1.5 %copy.18.step_raw = bf16[256,40]{1,0:T(8,128)(2,1)} copy(bf16[256,40]{0,1:T(8,128)(2,1)} %param.13) | data formatting | bytes 40960 | tf_op args[2]
  6.1 53.9 %shard_map.122 = (bf16[256,2560]{1,0:T(8,128)(2,1)}, f32[3,640,128]{2,1,0:T(8,128)}) custom-call(s32[4]{0:T(128)} %deal.1, s32[3]{0:T(128)} %lengths.1, bf16[256,2816]{1,0:T(8,128)(2,1)} %x.3, bf16[256,2560]{1,0:T(8,128)(2,1)} %gate.1, bf16[256,40]{1,0:T(8,128)(2,1)} %copy.18.step_raw, f32[4,2816]{1,0:T(4,128)} %conv_weight.1, ...), custom_call_target="tpu_custom_call" | custom-call | tf_op jit(solution)/shard_map/pallas_call | solution.py:623
  60.1 0.0 copy-start
  60.1 2.5 %copy.21 = bf16[256,2560]{1,0:T(8,128)(2,1)} copy(bf16[256,2560]{1,0:T(8,128)(2,1)} %get-tuple-element.4) | data formatting | bytes 2621440
  62.6 0.0 copy-done
  62.6 0.9 %copy.22 = f32[3,640,128]{2,1,0:T(8,128)} copy(f32[3,640,128]{2,1,0:T(8,128)S(1)} %copy-done) | data formatting | bytes 1966080
Async XLA Ops:
  60.1 2.6 %copy-start = (f32[3,640,128]{2,1,0:T(8,128)S(1)}, f32[3,640,128]{2,1,0:T(8,128)}, u32[]{:S(2)}) copy-start(f32[3,640,128]{2,1,0:T(8,128)} %get-tuple-element.5) | copy-start | bytes 2949124

commit v2 on v1

--- a/solution.py
+++ b/solution.py
@@ -206,6 +206,7 @@
 SLOT = QUARTER + STATE
 PAD = 48
 ROWS3 = 3 * PAD
+EARLY = 10
 LOG2E = 1.4426950408889634
 F32 = jnp.float32
 BF16 = jnp.bfloat16
@@ -250,14 +251,16 @@
     deal,
     lengths,
     x,
-    gate,
+    gate_hbm,
     step_raw,
     conv_weight,
     conv_bias,
-    heads_in,
+    step_bias_in,
+    rate_in,
+    skip_in,
     norm_gain,
     out,
-    finals,
+    finals_hbm,
     steps,
     tails,
     keys_raw,
@@ -281,6 +284,11 @@
     split_run,
     expand,
     keep_mask,
+    params,
+    per_head,
+    gate,
+    finals,
+    local_sem,
     send_sem,
     recv_sem,
 ):
@@ -292,11 +300,13 @@
             barrier, inc=1, device_id={"seq": peer}, device_id_type=pl.DeviceIdType.MESH
         )
 
-    eye = (
-        lax.broadcasted_iota(jnp.int32, (PAD, HEADS), 0)
-        == lax.broadcasted_iota(jnp.int32, (PAD, HEADS), 1)
+    gate_copy = pltpu.make_async_copy(gate_hbm, gate, local_sem.at[0])
+    gate_copy.start()
+    finals_copy = pltpu.make_async_copy(finals, finals_hbm, local_sem.at[1])
+
+    steps[me] = jnp.concatenate(
+        [step_raw[...].astype(F32), jnp.zeros((PAD - HEADS, STRETCH), F32)], 0
     ).astype(BF16)
-    steps[me] = nt(eye, step_raw[...]).astype(BF16)
     last = x[STRETCH - 16 :, :].astype(F32)[13:16, :]
     tail_f[0] = jnp.zeros((16, QUARTER), F32)
     for j in range(GROUP):
@@ -389,6 +399,15 @@
                 total_tail = total_tail + one_if(order[j] == order[i] - 1) * tail_f[j]
         lead[i] = total_tail
 
+    params[0:KERNEL] = conv_weight[...]
+    for c in range(CHANNELS // 128):
+        params[4:5, c * 128 : c * 128 + 128] = conv_bias[c * 128 : c * 128 + 128][None, :]
+    for c in range(INNER // 128):
+        params[5:6, c * 128 : c * 128 + 128] = norm_gain[c * 128 : c * 128 + 128][None, :]
+    per_head[...] = jnp.zeros((8, 128), F32)
+    for k, source in enumerate((step_bias_in, rate_in, skip_in)):
+        per_head[k : k + 1, 0:HEADS] = source[...]
+    heads_in = jnp.transpose(per_head[...])[0:PAD]
     step_bias = heads_in[:, 0:1]
     rate = heads_in[:, 1:2] * LOG2E
     upper = one_if(
@@ -423,8 +442,8 @@
     ext[5:8, INNER:] = lead[me, 12:15, 0 : 2 * STATE]
 
     def conv(source, cols, weight_cols):
-        taps = conv_weight[:, weight_cols]
-        value = conv_bias[:, weight_cols] + taps[KERNEL - 1 : KERNEL] * source[8 : 8 + STRETCH, cols]
+        taps = params[0:8, weight_cols]
+        value = taps[4:5] + taps[KERNEL - 1 : KERNEL] * source[8 : 8 + STRETCH, cols]
         for j in range(KERNEL - 1):
             value = value + taps[j : j + 1] * source[5 + j : 5 + j + STRETCH, cols] * keep_mask[j]
         return silu(value).astype(BF16)
@@ -484,7 +503,7 @@
     skip_split = split3(jnp.broadcast_to(heads_in[:, 2:3], (PAD, 128)))
     skip_rows = jnp.transpose(skip_split.astype(F32))[0:16].astype(BF16)
     masked_scores[...] = scores
-    lax.fori_loop(0, HEADS // 2, pair, 0)
+    lax.fori_loop(0, EARLY, pair, 0)
 
     spread_q = expand[:, quarter]
     for slot in (me,) + (partners[1], partners[2], partners[0]):
@@ -573,6 +592,10 @@
             inflow = inflow + ends_here * carried[c]
         finals[d] = state + by_row[:, GROUP * GROUP + d : GROUP * GROUP + d + 1] * inflow
 
+    finals_copy.start()
+    lax.fori_loop(EARLY, HEADS // 2, pair, 0)
+
+    gate_copy.wait()
     doc_lane = doc_of(lanes + mine * STRETCH)
     carry_t = jnp.where(doc_lane == prev_of(mine), jnp.exp2(log_run[me]), 0.0)
     carry_rows = jnp.transpose(split3(carry_t).astype(F32)).astype(BF16)
@@ -596,10 +619,11 @@
 
     def norm_chunk(c, carry):
         cols = pl.ds(pl.multiple_of(c * 128, 128), 128)
-        out[:, cols] = (y[:, cols] * factor * norm_gain[:, cols]).astype(BF16)
+        out[:, cols] = (y[:, cols] * factor * params[5:6, cols]).astype(BF16)
         return carry
 
     lax.fori_loop(0, INNER // 128, norm_chunk, 0)
+    finals_copy.wait()
     for copy in sends + back:
         copy.wait_send()
 
@@ -617,17 +641,17 @@
     skip_gain,
     norm_gain,
 ):
-    heads_in = jnp.pad(jnp.stack([step_bias, decay_rate, skip_gain], 1), ((0, PAD - HEADS), (0, 0)))
     smem = pl.BlockSpec(memory_space=pltpu.SMEM)
     vmem = pl.BlockSpec(memory_space=pltpu.VMEM)
+    anywhere = pl.BlockSpec(memory_space=pl.ANY)
     return pl.pallas_call(
         kernel,
         out_shape=(
             jax.ShapeDtypeStruct((STRETCH, INNER), BF16),
             jax.ShapeDtypeStruct((DOCS, QUARTER, STATE), F32),
         ),
-        in_specs=[smem, smem] + [vmem] * 7,
-        out_specs=(vmem, vmem),
+        in_specs=[smem, smem, vmem, anywhere] + [vmem] * 7,
+        out_specs=(vmem, anywhere),
         scratch_shapes=[
             pltpu.VMEM((GROUP, PAD, STRETCH), BF16),
             pltpu.VMEM((GROUP, 16, QUARTER), BF16),
@@ -652,6 +676,11 @@
             pltpu.VMEM((ROWS3, STRETCH), BF16),
             pltpu.VMEM((ROWS3, INNER), BF16),
             pltpu.VMEM((KERNEL - 1, STRETCH, 128), F32),
+            pltpu.VMEM((8, CHANNELS), F32),
+            pltpu.VMEM((8, 128), F32),
+            pltpu.VMEM((STRETCH, INNER), BF16),
+            pltpu.VMEM((DOCS, QUARTER, STATE), F32),
+            pltpu.SemaphoreType.DMA((2,)),
             pltpu.SemaphoreType.DMA((5, GROUP)),
             pltpu.SemaphoreType.DMA((5, GROUP)),
         ],
@@ -663,11 +692,13 @@
         lengths,
         mixer_in,
         gate_input,
-        step_raw,
+        step_raw.T,
         conv_weight,
-        conv_bias[None, :],
-        heads_in,
-        norm_gain[None, :],
+        conv_bias,
+        step_bias[None, :],
+        decay_rate[None, :],
+        skip_gain[None, :],
+        norm_gain,
     )
 
 

time: 63.9 us -> 53.3 us (0.83)
  Pallas kernels: 53.9 us -> 49 us
  local copies, waits for them, and re-layouts: 8.27 us -> 3.49 us
  other arithmetic: 0.7 us -> 0 us
    pallas_call x1, Pallas kernels: 53.9 us -> 49 us  [fused(): pl.pallas_call(kernel, out_shape=(jax.ShapeDtypeStruct((STRETCH, INNER),...]
    broadcast_in_dim x2 -> x0, local copies, waits for them, and re-layouts: 2.61 us -> none  [the longest x1 1.31 us: fused(): norm_gain[None, :]]
    unnamed x5 -> x4, local copies, waits for them, and re-layouts: 4.95 us -> 3.49 us
    another operation x1 -> x0, other arithmetic: 0.7 us -> none  [fused(): jnp.stack([step_bias, decay_rate, skip_gain], 1)]
where the time goes in v2:
time: 53.3 us; the launch traced here: 53.2 us
  Pallas kernels  49 us (92%)
  local copies, waits for them, and re-layouts  3.49 us (7%)
  between operations  0.65 us (1%)
    pallas_call x1, Pallas kernels, fused(): pl.pallas_call(kernel, out_shape=(jax.ShapeDtypeStruct((STRETCH, INNER),...  49 us
    unnamed x4, local copies, waits for them, and re-layouts  3.49 us

profile of v2, /device:TPU:0, one launch (start us, length us, event | category | flops | bytes accessed | tf_op | source)
XLA Modules:
  0.0 53.2 jit_solution(7942512002470170303)
XLA Ops:
  0.6 49.0 %shard_map.122 = (bf16[256,2560]{1,0:T(8,128)(2,1)}, f32[3,640,128]{2,1,0:T(8,128)}) custom-call(s32[4]{0:T(128)} %deal.1, s32[3]{0:T(128)} %lengths.1, bf16[256,2816]{1,0:T(8,128)(2,1)} %x.1, bf16[256,2560]{1,0:T(8,128)(2,1)} %gate_hbm.1, bf16[40,256]{1,0:T(8,128)(2,1)} %bitcast.4, f32[4,2816]{1,0:T(4,128)} %conv_weight.1, f32[2816]{0:T(1024)} %conv_bias.1, ...), custom_call_target="tpu_custom_call" | custom-call | tf_op jit(solution)/shard_map/pallas_call | solution.py:647
  49.7 0.0 copy-start
  49.7 2.5 %copy.15 = bf16[256,2560]{1,0:T(8,128)(2,1)} copy(bf16[256,2560]{1,0:T(8,128)(2,1)} %get-tuple-element.4) | data formatting | bytes 2621440
  52.2 0.0 copy-done
  52.2 0.9 %copy.16 = f32[3,640,128]{2,1,0:T(8,128)} copy(f32[3,640,128]{2,1,0:T(8,128)S(1)} %copy-done) | data formatting | bytes 1966080
Async XLA Ops:
  49.7 2.6 %copy-start = (f32[3,640,128]{2,1,0:T(8,128)S(1)}, f32[3,640,128]{2,1,0:T(8,128)}, u32[]{:S(2)}) copy-start(f32[3,640,128]{2,1,0:T(8,128)} %get-tuple-element.5) | copy-start | bytes 2949124

commit v3 on v2

--- a/solution.py
+++ b/solution.py
@@ -454,7 +454,7 @@
         mixed[:, cols] = conv(ext, cols, cols)
         return carry
 
-    lax.fori_loop(0, CHANNELS // 128, own_chunk, 0)
+    lax.fori_loop(0, CHANNELS // 128, own_chunk, 0, unroll=2)
 
     step_rows = jnp.transpose(split3(step_t[me]).astype(F32)).astype(BF16)
     keys = mixed[:, INNER : INNER + STATE]
@@ -503,7 +503,7 @@
     skip_split = split3(jnp.broadcast_to(heads_in[:, 2:3], (PAD, 128)))
     skip_rows = jnp.transpose(skip_split.astype(F32))[0:16].astype(BF16)
     masked_scores[...] = scores
-    lax.fori_loop(0, EARLY, pair, 0)
+    lax.fori_loop(0, EARLY, pair, 0, unroll=2)
 
     spread_q = expand[:, quarter]
     for slot in (me,) + (partners[1], partners[2], partners[0]):
@@ -593,7 +593,7 @@
         finals[d] = state + by_row[:, GROUP * GROUP + d : GROUP * GROUP + d + 1] * inflow
 
     finals_copy.start()
-    lax.fori_loop(EARLY, HEADS // 2, pair, 0)
+    lax.fori_loop(EARLY, HEADS // 2, pair, 0, unroll=2)
 
     gate_copy.wait()
     doc_lane = doc_of(lanes + mine * STRETCH)
@@ -622,7 +622,7 @@
         out[:, cols] = (y[:, cols] * factor * params[5:6, cols]).astype(BF16)
         return carry
 
-    lax.fori_loop(0, INNER // 128, norm_chunk, 0)
+    lax.fori_loop(0, INNER // 128, norm_chunk, 0, unroll=2)
     finals_copy.wait()
     for copy in sends + back:
         copy.wait_send()

time: 53.3 us -> 50.8 us (0.953)
  Pallas kernels: 49 us -> 46.5 us
    pallas_call x1, Pallas kernels: 49 us -> 46.5 us  [fused(): pl.pallas_call(kernel, out_shape=(jax.ShapeDtypeStruct((STRETCH, INNER),...]
where the time goes in v3:
time: 50.8 us; the launch traced here: 50.7 us
  Pallas kernels  46.5 us (92%)
  local copies, waits for them, and re-layouts  3.49 us (7%)
  between operations  0.65 us (1%)
    pallas_call x1, Pallas kernels, fused(): pl.pallas_call(kernel, out_shape=(jax.ShapeDtypeStruct((STRETCH, INNER),...  46.5 us
    unnamed x4, local copies, waits for them, and re-layouts  3.49 us

profile of v3, /device:TPU:0, one launch (start us, length us, event | category | flops | bytes accessed | tf_op | source)
XLA Modules:
  0.0 50.7 jit_solution(1585681532686857340)
XLA Ops:
  0.6 46.5 %shard_map.122 = (bf16[256,2560]{1,0:T(8,128)(2,1)}, f32[3,640,128]{2,1,0:T(8,128)}) custom-call(s32[4]{0:T(128)} %deal.1, s32[3]{0:T(128)} %lengths.1, bf16[256,2816]{1,0:T(8,128)(2,1)} %x.1, bf16[256,2560]{1,0:T(8,128)(2,1)} %gate_hbm.1, bf16[40,256]{1,0:T(8,128)(2,1)} %bitcast.4, f32[4,2816]{1,0:T(4,128)} %conv_weight.1, f32[2816]{0:T(1024)} %conv_bias.1, ...), custom_call_target="tpu_custom_call" | custom-call | tf_op jit(solution)/shard_map/pallas_call | solution.py:647
  47.2 0.0 copy-start
  47.2 2.5 %copy.15 = bf16[256,2560]{1,0:T(8,128)(2,1)} copy(bf16[256,2560]{1,0:T(8,128)(2,1)} %get-tuple-element.4) | data formatting | bytes 2621440
  49.7 0.0 copy-done
  49.7 0.9 %copy.16 = f32[3,640,128]{2,1,0:T(8,128)} copy(f32[3,640,128]{2,1,0:T(8,128)S(1)} %copy-done) | data formatting | bytes 1966080
Async XLA Ops:
  47.2 2.6 %copy-start = (f32[3,640,128]{2,1,0:T(8,128)S(1)}, f32[3,640,128]{2,1,0:T(8,128)}, u32[]{:S(2)}) copy-start(f32[3,640,128]{2,1,0:T(8,128)} %get-tuple-element.5) | copy-start | bytes 2949124
